TPU v7x, 128 devices: a whole 4x4x4 slice. The times are simulated.
128 devices in a mesh: head: 4 (over x), seq: 32 (over y, z, core).
Axes of the slice: x: 4, y: 4, z: 4, core: 2. Of those that a mesh axis runs over, the one named last changes fastest.
Arguments:
- queries: bfloat16 [16384, 8192], P('seq', 'head'), may hold values from -200 to 200
- keys: bfloat16 [16384, 8192], P('seq', 'head'), may hold values from -6 to 6
- values: bfloat16 [16384, 8192], P('seq', 'head'), may hold values from -6 to 6
- cotangent: bfloat16 [16384, 8192], P('seq', 'head'), may hold values from -6 to 6
- prefix_keys: bfloat16 [16384, 8192], P('seq', 'head'), may hold values from -1.5 to 1.5
- prefix_values: bfloat16 [16384, 8192], P('seq', 'head'), may hold values from -1.5 to 1.5
- gain: float32 [8192], P('head'), may hold values from 0.5 to 1.5
- lengths: int32 [32], P('seq'), may hold values from 64 to 512, as said below
Outputs:
- normed: bfloat16 [16384, 8192], P('seq', 'head')
- query_grad: bfloat16 [16384, 8192], P('seq', 'head')
- key_grad: bfloat16 [16384, 8192], P('seq', 'head')
- value_grad: bfloat16 [16384, 8192], P('seq', 'head')
- prefix_key_grad: bfloat16 [16384, 8192], P('seq', 'head')
- prefix_value_grad: bfloat16 [16384, 8192], P('seq', 'head')
Inputs may be any that keep to these rules, and one draw needn't show every extreme that they name: `lengths`: one length per response; some response has exactly 512 live slots and some exactly 64.
All inputs are finite; a program needn't handle non-finite values.
Results may differ from a plain program's by a relative error of at most 0.0058.
Values sent between devices are 32-bit elements; how exact they have to be, the bound alone decides.
No kernel may reach another device: no remote copies, remote signals or barrier semaphores. Data moves between devices by JAX's collectives and lax.ppermute only.
A program may use at most 128 MiB of HBM per device.

v0:
```python
import functools
import jax
import jax.numpy as jnp
from jax import lax
from jax.sharding import PartitionSpec as P

H = 64
HEAD_DIM = 128
BLOCK = 256
epsilon = 1e-06


def summed_prefix(partial_state):
    return lax.psum(partial_state, "seq")


def body(queries, keys, values, cotangent, prefix_keys, prefix_values, gain, lengths):
    tok_rows, tok_cols = queries.shape
    heads_here = tok_cols // HEAD_DIM
    block_count = tok_rows // BLOCK
    length = lengths[0]
    is_live = lax.iota(jnp.int32, tok_rows) < length
    live_mask = is_live.astype(jnp.bfloat16)[:, None]
    block_shape = (block_count, BLOCK, heads_here, HEAD_DIM)
    q_live = (queries * live_mask).reshape(block_shape)
    k_live = (keys * live_mask).reshape(block_shape)
    v_live = (values * live_mask).reshape(block_shape)
    causal = (lax.iota(jnp.int32, BLOCK)[:, None] >= lax.iota(jnp.int32, BLOCK)[None, :]).astype(
        jnp.float32
    )
    pre_keys = prefix_keys.reshape(-1, heads_here, HEAD_DIM)
    pre_values = prefix_values.reshape(-1, heads_here, HEAD_DIM)
    partial_state = jnp.einsum(
        "thd,the->hde", pre_keys, pre_values, preferred_element_type=jnp.float32
    )

    def intra_block(index):
        q_block = q_live[index]
        k_block = k_live[index]
        v_block = v_live[index]
        scores = jnp.einsum("bhd,shd->hbs", q_block, k_block, preferred_element_type=jnp.float32)
        scores = (scores * causal).astype(jnp.bfloat16)
        in_block = jnp.einsum("hbs,she->bhe", scores, v_block, preferred_element_type=jnp.float32)
        block_kv = jnp.einsum("bhd,bhe->hde", k_block, v_block, preferred_element_type=jnp.float32)
        return (in_block, scores, block_kv)

    def from_state_of(index, state_bf):
        return jnp.einsum(
            "bhd,hde->bhe", q_live[index], state_bf, preferred_element_type=jnp.float32
        )

    results = []
    score_list = []
    state_list = []
    prefix_state = summed_prefix(partial_state)

    def forward_block(index, state_now):
        state_bf = state_now.astype(jnp.bfloat16)
        in_block, scores, block_kv = intra_block(index)
        return (from_state_of(index, state_bf) + in_block, scores, state_bf, state_now + block_kv)

    state_now = prefix_state
    for index in range(block_count):
        step_fn = functools.partial(forward_block, index)
        packed = step_fn(state_now)
        results.append(packed[0])
        score_list.append(packed[1])
        state_list.append(packed[2])
        state_now = packed[3]
    attended = jnp.concatenate(results, axis=0).reshape(tok_rows, tok_cols)
    scaled_cot = gain * (cotangent * live_mask).astype(jnp.float32)
    square_sum, inner_sum = lax.psum(
        (jnp.sum(attended * attended, axis=1), jnp.sum(scaled_cot * attended, axis=1)), "head"
    )
    root_mean = jnp.sqrt(square_sum / (H * HEAD_DIM) + epsilon)[:, None]
    inner_sum = inner_sum[:, None]
    normed = (gain * attended / root_mean).astype(jnp.bfloat16)
    out_grad = scaled_cot / root_mean - attended * inner_sum / (H * HEAD_DIM * root_mean**3)
    out_grad = out_grad.astype(jnp.bfloat16).reshape(block_shape)

    def backward_block(index, grad_state):
        q_block = q_live[index]
        k_block = k_live[index]
        v_block = v_live[index]
        d_block = out_grad[index]
        scores = score_list[index]
        state_bf = state_list[index]
        grad_bf = grad_state.astype(jnp.bfloat16)
        pscore = jnp.einsum("bhe,she->hbs", d_block, v_block, preferred_element_type=jnp.float32)
        pscore = (pscore * causal).astype(jnp.bfloat16)
        grad_q = jnp.einsum(
            "bhe,hde->bhd", d_block, state_bf, preferred_element_type=jnp.float32
        ) + jnp.einsum("hbs,shd->bhd", pscore, k_block, preferred_element_type=jnp.float32)
        grad_k = jnp.einsum(
            "bhe,hde->bhd", v_block, grad_bf, preferred_element_type=jnp.float32
        ) + jnp.einsum("hbs,bhd->shd", pscore, q_block, preferred_element_type=jnp.float32)
        grad_v = jnp.einsum(
            "bhd,hde->bhe", k_block, grad_bf, preferred_element_type=jnp.float32
        ) + jnp.einsum("hbs,bhe->she", scores, d_block, preferred_element_type=jnp.float32)
        grad_next = grad_state + jnp.einsum(
            "bhd,bhe->hde", q_block, d_block, preferred_element_type=jnp.float32
        )
        return (
            grad_q.astype(jnp.bfloat16),
            grad_k.astype(jnp.bfloat16),
            grad_v.astype(jnp.bfloat16),
            grad_next,
        )

    grad_state = jnp.zeros((heads_here, HEAD_DIM, HEAD_DIM), jnp.float32)
    query_parts = []
    key_parts = []
    value_parts = []
    for index in reversed(range(block_count)):
        step_fn = functools.partial(backward_block, index)
        packed = step_fn(grad_state)
        query_parts.insert(0, packed[0])
        key_parts.insert(0, packed[1])
        value_parts.insert(0, packed[2])
        grad_state = packed[3]
    total_grad = lax.psum(grad_state, "seq")
    wide_keys = pre_keys.astype(jnp.float32)
    wide_values = pre_values.astype(jnp.float32)
    prefix_key_grad = jnp.einsum(
        "the,hde->thd", wide_values, total_grad, precision=lax.Precision.HIGHEST
    )
    prefix_value_grad = jnp.einsum(
        "thd,hde->the", wide_keys, total_grad, precision=lax.Precision.HIGHEST
    )
    query_grad = jnp.concatenate(query_parts, axis=0).reshape(tok_rows, tok_cols)
    key_grad = jnp.concatenate(key_parts, axis=0).reshape(tok_rows, tok_cols)
    value_grad = jnp.concatenate(value_parts, axis=0).reshape(tok_rows, tok_cols)
    return (
        normed,
        query_grad,
        key_grad,
        value_grad,
        prefix_key_grad.astype(jnp.bfloat16).reshape(prefix_keys.shape),
        prefix_value_grad.astype(jnp.bfloat16).reshape(prefix_values.shape),
    )


def solution(mesh):
    return jax.shard_map(
        body,
        mesh=mesh,
        in_specs=(
            P("seq", "head"),
            P("seq", "head"),
            P("seq", "head"),
            P("seq", "head"),
            P("seq", "head"),
            P("seq", "head"),
            P("head"),
            P("seq"),
        ),
        out_specs=(
            P("seq", "head"),
            P("seq", "head"),
            P("seq", "head"),
            P("seq", "head"),
            P("seq", "head"),
            P("seq", "head"),
        ),
        check_vma=False,
    )
```

profile of v0, /device:TPU:1, one launch (start us, length us, event | category | flops | bytes accessed | tf_op | source)
XLA Modules:
  0.0 292.5 jit_solution(10290730926463739367)
XLA Ops:
  7.2 1.5 copy-done
  8.8 3.4 %fusion.8 = f32[16,128,128]{2,1,0:T(8,128)} fusion(bf16[512,2048]{1,0:T(8,128)(2,1)} %param.13, bf16[512,2048]{1,0:T(8,128)(2,1)S(1)} %copy-done), kind=kOutput, calls=%fused_computation.18 | convolution fusion | flops 268435456 | bytes 5242880 | tf_op jit(solution)/shard_map/thd,the->hde/dot_general | solution.py:33
  13.0 3.9 %copy.49 = bf16[512,2048]{0,1:T(8,128)(2,1)} copy(bf16[512,2048]{1,0:T(8,128)(2,1)} %param.8) | data formatting | bytes 4194304 | tf_op args[0]
  16.9 3.9 %copy.53 = bf16[512,2048]{0,1:T(8,128)(2,1)} copy(bf16[512,2048]{1,0:T(8,128)(2,1)} %param.9) | data formatting | bytes 4194304 | tf_op args[1]
  20.8 3.9 %copy.52 = bf16[512,2048]{0,1:T(8,128)(2,1)} copy(bf16[512,2048]{1,0:T(8,128)(2,1)} %param.10) | data formatting | bytes 4194304 | tf_op args[2]
  24.7 3.3 %broadcast_multiply_fusion = (bf16[512,2048]{0,1:T(8,128)(2,1)S(1)}, bf16[512,2048]{0,1:T(8,128)(2,1)S(1)}, bf16[512,2048]{0,1:T(8,128)(2,1)S(1)}) fusion(bf16[512,2048]{0,1:T(8,128)(2,1)} %copy.53, bf16[512]{0:T(512)(128)(2,1)S(1)} %fusion.38, bf16[512,2048]{0,1:T(8,128)(2,1)} %copy.52, bf16[512,2048]{0,1:T(8,128)(2,1)} %copy.49), kind=kLoop, calls=%fused_computation.49 | loop fusion | flops 3145728 | bytes 12583936 | tf_op jit(solution)/shard_map/mul | solution.py:26
  30.8 2.2 fusion.45
  33.0 2.1 multiply_convert_fusion.2
  35.1 3.9 %copy.61 = bf16[512,2048]{0,1:T(8,128)(2,1)} copy(bf16[512,2048]{1,0:T(8,128)(2,1)} %param.11) | data formatting | bytes 4194304 | tf_op args[3]
  39.0 4.1 %fusion.46 = f32[16,128,256]{2,1,0:T(8,128)} fusion(bf16[256,16,128]{0,2,1:T(8,128)(2,1)} %bitcast.148, bf16[16,256,256]{2,1,0:T(8,128)(2,1)} %multiply_convert_fusion.2), kind=kOutput, calls=%fused_computation.72 | convolution fusion | flops 268435456 | bytes 5242880 | tf_op jit(solution)/shard_map/hbs,she->bhe/dot_general | solution.py:43
  43.0 77.5 %all-reduce.4.cloned.1.call-done = f32[16,128,128]{2,1,0:T(8,128)} async-done(((f32[16,128,128]{2,1,0:T(8,128)}), f32[16,128,128]{2,1,0:T(8,128)}) %all-reduce.4.cloned.1.call-update) | async-done | bytes 1048592 | tf_op jit(solution)/shard_map/psum | solution.py:14
  120.5 2.1 fusion.29
  128.5 8.7 %all-reduce = (f32[512]{0:T(512)S(1)}, f32[512]{0:T(512)S(1)}) all-reduce(f32[512]{0:T(512)S(1)} %get-tuple-element.22, f32[512]{0:T(512)S(1)} %fusion.2), channel_id=1, replica_groups=mesh['head'=4,'seq'=32] {'head'}, use_global_device_ids=true, to_apply=%region_2.0 | all-reduce | flops 1024 | bytes 8192 | tf_op jit(solution)/shard_map/psum | solution.py:72
  137.3 4.5 %fusion.5 = (bf16[512,2048]{0,1:T(8,128)(2,1)S(1)}, bf16[512,2048]{0,1:T(8,128)(2,1)}) fusion(f32[512,16,128]{0,2,1:T(8,128)} %copy-done.1, f32[512]{0:T(512)S(1)} %get-tuple-element.32, f32[512]{0:T(512)S(1)} %get-tuple-element.19, f32[512]{0:T(512)S(1)} %get-tuple-element.33, f32[2048]{0:T(1024)S(1)} %copy-done.35, bf16[512,2048]{0,1:T(8,128)(2,1)} %copy.61, ...), kind=kLoop, calls=%fused_computation.9 | loop fusion | flops 11534336 | bytes 10501120 | tf_op jit(solution)/shard_map/convert_element_type | solution.py:79
  141.9 2.2 copy-done.18
  147.4 1.8 fusion.51
  149.1 2.1 fusion.48
  151.3 1.8 fusion.52
  154.3 1.8 fusion.50
  156.1 2.1 fusion.47
  161.1 3.4 %fusion.27 = bf16[256,16,128]{0,2,1:T(8,128)(2,1)} fusion(f32[16,128,256]{2,1,0:T(8,128)} %fusion.52, bf16[256,16,128]{0,2,1:T(8,128)(2,1)S(1)} %bitcast.124, f32[16,128,128]{2,1,0:T(8,128)} %copy-done.19), kind=kOutput, calls=%fused_computation.44 | convolution fusion | flops 135528448 | bytes 5242880 | tf_op jit(solution)/shard_map/bhd,hde->bhe/dot_general | solution.py:97
  164.5 3.6 %fusion.26 = bf16[256,16,128]{0,2,1:T(8,128)(2,1)} fusion(f32[16,128,256]{2,1,0:T(8,128)} %fusion.51, bf16[256,16,128]{0,2,1:T(8,128)(2,1)} %bitcast.149), kind=kOutput, calls=%fused_computation.43 | convolution fusion | flops 135266304 | bytes 4194304 | tf_op jit(solution)/shard_map/bhe,hde->bhd/dot_general | solution.py:94
  174.6 3.9 %copy.82 = bf16[512,2048]{1,0:T(8,128)(2,1)} copy(bf16[512,2048]{0,1:T(8,128)(2,1)} %bitcast.151) | data formatting | bytes 4194304
  178.6 4.0 %copy.80 = bf16[512,2048]{1,0:T(8,128)(2,1)} copy(bf16[512,2048]{0,1:T(8,128)(2,1)} %bitcast.152) | data formatting | bytes 4194304
  182.6 2.4 fusion.25
  186.6 3.9 %copy.81 = bf16[512,2048]{1,0:T(8,128)(2,1)} copy(bf16[512,2048]{0,1:T(8,128)(2,1)} %bitcast.153) | data formatting | bytes 4194304
  190.5 3.9 %copy.79 = bf16[512,2048]{1,0:T(8,128)(2,1)} copy(bf16[512,2048]{0,1:T(8,128)(2,1)} %get-tuple-element.21) | data formatting | bytes 4194304
  194.4 74.1 %all-reduce.6.cloned.1.call-done = f32[16,128,128]{2,1,0:T(8,128)} async-done(((f32[16,128,128]{2,1,0:T(8,128)}), f32[16,128,128]{2,1,0:T(8,128)}) %all-reduce.6.cloned.1.call-update) | async-done | bytes 1048592 | tf_op jit(solution)/shard_map/psum | solution.py:121
  268.5 4.4 %fusion.13 = bf16[16,128,512]{2,1,0:T(8,128)(2,1)} fusion(f32[16,128,128]{2,1,0:T(8,128)} %all-reduce.6.cloned.1.call-done, bf16[512,2048]{1,0:T(8,128)(2,1)S(1)} %copy-done), kind=kOutput, calls=%fused_computation.34 | convolution fusion | flops 1611661312 | bytes 5242880 | tf_op jit(solution)/shard_map/thd,hde->the/dot_general | solution.py:127
  273.0 4.0 %copy.84 = bf16[512,2048]{1,0:T(8,128)(2,1)} copy(bf16[512,2048]{0,1:T(8,128)(2,1)} %bitcast.155) | data formatting | bytes 4194304
  277.0 4.8 %fusion.16 = bf16[16,128,512]{2,1,0:T(8,128)(2,1)} fusion(f32[16,128,128]{2,1,0:T(8,128)S(1)} %copy-done.31, bf16[512,2048]{1,0:T(8,128)(2,1)} %param.13), kind=kOutput, calls=%fused_computation.35 | convolution fusion | flops 1611661312 | bytes 5242880 | tf_op jit(solution)/shard_map/the,hde->thd/dot_general | solution.py:124
  281.7 3.9 %copy.83 = bf16[512,2048]{1,0:T(8,128)(2,1)} copy(bf16[512,2048]{0,1:T(8,128)(2,1)} %bitcast.154) | data formatting | bytes 4194304
  (96 shorter events, 24.3 us)
Async XLA Ops:
  7.2 1.6 copy-start
  7.2 113.3 %all-reduce.4.cloned.1.call-start = ((), (), s32[]{:S(2)}) async-start(), calls=%async_computation | async-start | bytes 2097152 | tf_op jit(solution)/shard_map/psum | solution.py:14
  12.2 256.3 %all-reduce.6.cloned.1.call-start = ((), (), s32[]{:S(2)}) async-start(), calls=%async_computation.1 | async-start | bytes 2097152 | tf_op jit(solution)/shard_map/psum | solution.py:121
  28.1 4.8 %copy-start.20 = (bf16[256,2048]{0,1:T(8,128)(2,1)}, bf16[256,2048]{0,1:T(8,128)(2,1)S(1)}, u32[]{:S(2)}) copy-start(bf16[256,2048]{0,1:T(8,128)(2,1)S(1)} %get-tuple-element.31) | copy-start | bytes 3145732
  29.4 1.4 copy-start.2
  29.4 3.5 %copy-start.9 = (bf16[256,2048]{0,1:T(8,128)(2,1)}, bf16[256,2048]{0,1:T(8,128)(2,1)S(1)}, u32[]{:S(2)}) copy-start(bf16[256,2048]{0,1:T(8,128)(2,1)S(1)} %get-tuple-element.27) | copy-start | bytes 3145732
  30.4 2.5 copy-start.16
  120.5 2.1 copy-start.10
  120.5 2.5 copy-start.28
  123.1 1.4 copy-start.13
  123.1 1.7 copy-start.23
  123.1 2.4 copy-start.25
  126.0 1.7 copy-start.15
  126.0 1.7 copy-start.35
  126.5 2.0 copy-start.1
  141.8 2.3 copy-start.18
  141.9 3.9 %copy-start.7 = (bf16[256,2048]{0,1:T(8,128)(2,1)}, bf16[256,2048]{0,1:T(8,128)(2,1)S(1)}, u32[]{:S(2)}) copy-start(bf16[256,2048]{0,1:T(8,128)(2,1)S(1)} %get-tuple-element.25) | copy-start | bytes 3145732
  141.9 17.7 %copy-start.5 = (bf16[256,2048]{0,1:T(8,128)(2,1)}, bf16[256,2048]{0,1:T(8,128)(2,1)S(1)}, u32[]{:S(2)}) copy-start(bf16[256,2048]{0,1:T(8,128)(2,1)S(1)} %get-tuple-element.24) | copy-start | bytes 3145732
  146.6 13.1 %copy-start.19 = (f32[16,128,128]{2,1,0:T(8,128)}, f32[16,128,128]{2,1,0:T(8,128)S(1)}, u32[]{:S(2)}) copy-start(f32[16,128,128]{2,1,0:T(8,128)S(1)} %fusion.49) | copy-start | bytes 3145732
  147.3 1.8 copy-start.21
  149.1 2.1 copy-start.17
  151.3 1.8 copy-start.3
  164.5 3.6 %copy-start.8 = (bf16[256,2048]{0,1:T(8,128)(2,1)S(1)}, bf16[256,2048]{0,1:T(8,128)(2,1)}, u32[]{:S(2)}) copy-start(bf16[256,2048]{0,1:T(8,128)(2,1)} %copy-done.7) | copy-start | bytes 3145732
  164.5 3.6 %copy-start.26 = (f32[16,128,256]{2,1,0:T(8,128)S(1)}, f32[16,128,256]{2,1,0:T(8,128)}, u32[]{:S(2)}) copy-start(f32[16,128,256]{2,1,0:T(8,128)} %fusion.48) | copy-start | bytes 6291460
  164.5 3.6 %copy-start.30 = (bf16[16,128,128]{2,1,0:T(8,128)(2,1)S(1)}, bf16[16,128,128]{2,1,0:T(8,128)(2,1)}, u32[]{:S(2)}) copy-start(bf16[16,128,128]{2,1,0:T(8,128)(2,1)} %copy-done.29) | copy-start | bytes 1572868
  168.1 1.5 copy-start.34
  169.6 1.5 copy-start.6
  169.6 2.3 copy-start.24
  169.6 3.1 %copy-start.27 = (f32[16,128,256]{2,1,0:T(8,128)S(1)}, f32[16,128,256]{2,1,0:T(8,128)}, u32[]{:S(2)}) copy-start(f32[16,128,256]{2,1,0:T(8,128)} %fusion.47) | copy-start | bytes 6291460
  178.6 4.0 %copy-start.4 = (bf16[256,2048]{0,1:T(8,128)(2,1)S(1)}, bf16[256,2048]{0,1:T(8,128)(2,1)}, u32[]{:S(2)}) copy-start(bf16[256,2048]{0,1:T(8,128)(2,1)} %copy-done.2) | copy-start | bytes 3145732
  182.6 2.5 copy-start.33
  272.9 4.0 %copy-start.31 = (f32[16,128,128]{2,1,0:T(8,128)S(1)}, f32[16,128,128]{2,1,0:T(8,128)}, u32[]{:S(2)}) copy-start(f32[16,128,128]{2,1,0:T(8,128)} %all-reduce.6.cloned.1.call-done) | copy-start | bytes 3145732
  (6 other events, 6.7 us)
Sparse Core Ops, SparseCore 0:
  12.3 108.1 all-reduce.3
  164.6 103.9 all-reduce.5
where the time goes:
time: 294 us; the launch traced here: 292 us
  waiting for transfers between devices  152 us (52%)
  local copies, waits for them, and re-layouts  53.5 us (18%)
  matrix products  50 us (17%)
  between operations  15 us (5%)
  other arithmetic  13.6 us (5%)
  blocking collectives  8.75 us (3%)
    psum x1, waiting for transfers between devices, summed_prefix(): return lax.psum(partial_state, 'seq')  77.5 us
    psum x1, waiting for transfers between devices, body(): total_grad = lax.psum(grad_state, 'seq')  74.1 us
    unnamed x82, local copies, waits for them, and re-layouts  52 us
    psum x1, blocking collectives, body(): lax.psum((jnp.sum(attended * attended, axis=1), jnp.sum(scaled_cot * atte...  8.75 us
    dot_general x2, matrix products, intra_block(): jnp.einsum('hbs,she->bhe', scores, v_block, preferred_element_type=jnp.fl...  6.21 us
    dot_general x2, matrix products, backward_block(): jnp.einsum('bhe,hde->bhd', v_block, grad_bf, preferred_element_type=jnp.f...  6.01 us
  transfers between devices with their start and end apart: 2, of which 2 were waited for; matrix products, arithmetic and copies ran while one was open for 19% of the time, Pallas kernels for 0%

commit v1 on v0

--- a/solution.py
+++ b/solution.py
@@ -11,7 +11,7 @@
 
 
 def summed_prefix(partial_state):
-    return lax.psum(partial_state, "seq")
+    return jnp.sum(lax.all_gather(partial_state, "seq"), axis=0)
 
 
 def body(queries, keys, values, cotangent, prefix_keys, prefix_values, gain, lengths):

time: 294 us -> 315 us (1.071)
  waiting for transfers between devices: 152 us -> 165 us
  other arithmetic: 13.6 us -> 26.2 us
    all_gather x0 -> x1, waiting for transfers between devices: none -> 90.9 us  [summed_prefix(): return jnp.sum(lax.all_gather(partial_state, 'seq'), axis=0)]
    psum x1 -> x0, waiting for transfers between devices: 77.5 us -> none  [summed_prefix(): return lax.psum(partial_state, 'seq')]
    reduce_sum x0 -> x1, other arithmetic: none -> 12.7 us  [summed_prefix(): return jnp.sum(lax.all_gather(partial_state, 'seq'), axis=0)]
    unnamed x82 -> x84, local copies, waits for them, and re-layouts: 52 us -> 50.5 us
  transfers between devices with their start and end apart: 2 -> 2, of which waited for: 2 -> 2; matrix products, arithmetic and copies ran while one was open for 19% -> 17% of each run, Pallas kernels for 0% -> 0%
where the time goes in v1:
time: 315 us; the launch traced here: 314 us
  waiting for transfers between devices  165 us (52%)
  local copies, waits for them, and re-layouts  51.1 us (16%)
  matrix products  48.5 us (15%)
  other arithmetic  26.2 us (8%)
  between operations  15 us (5%)
  blocking collectives  8.55 us (3%)
    all_gather x1, waiting for transfers between devices, summed_prefix(): return jnp.sum(lax.all_gather(partial_state, 'seq'), axis=0)  90.9 us
    psum x1, waiting for transfers between devices, body(): total_grad = lax.psum(grad_state, 'seq')  73.7 us
    unnamed x84, local copies, waits for them, and re-layouts  50.5 us
    reduce_sum x1, other arithmetic, summed_prefix(): return jnp.sum(lax.all_gather(partial_state, 'seq'), axis=0)  12.7 us
    psum x1, blocking collectives, body(): lax.psum((jnp.sum(attended * attended, axis=1), jnp.sum(scaled_cot * atte...  8.55 us
  transfers between devices with their start and end apart: 2, of which 2 were waited for; matrix products, arithmetic and copies ran while one was open for 17% of the time, Pallas kernels for 0%

profile of v1, /device:TPU:1, one launch (start us, length us, event | category | flops | bytes accessed | tf_op | source)
XLA Modules:
  0.0 314.1 jit_solution(8562278795867100948)
XLA Ops:
  8.8 3.4 %fusion.8 = f32[16,128,128]{2,1,0:T(8,128)} fusion(bf16[512,2048]{1,0:T(8,128)(2,1)} %param.13, bf16[512,2048]{1,0:T(8,128)(2,1)S(1)} %copy-done), kind=kOutput, calls=%fused_computation.18 | convolution fusion | flops 268435456 | bytes 5242880 | tf_op jit(solution)/shard_map/thd,the->hde/dot_general | solution.py:33
  12.9 3.9 %copy.99 = bf16[512,2048]{0,1:T(8,128)(2,1)} copy(bf16[512,2048]{1,0:T(8,128)(2,1)} %param.11) | data formatting | bytes 4194304 | tf_op args[3]
  16.9 3.9 %copy.87 = bf16[512,2048]{0,1:T(8,128)(2,1)} copy(bf16[512,2048]{1,0:T(8,128)(2,1)} %param.8) | data formatting | bytes 4194304 | tf_op args[0]
  20.8 3.9 %copy.91 = bf16[512,2048]{0,1:T(8,128)(2,1)} copy(bf16[512,2048]{1,0:T(8,128)(2,1)} %param.9) | data formatting | bytes 4194304 | tf_op args[1]
  24.7 4.1 %copy.90 = bf16[512,2048]{0,1:T(8,128)(2,1)} copy(bf16[512,2048]{1,0:T(8,128)(2,1)} %param.10) | data formatting | bytes 4194304 | tf_op args[2]
  28.8 3.3 %broadcast_multiply_fusion = (bf16[512,2048]{0,1:T(8,128)(2,1)S(1)}, bf16[512,2048]{0,1:T(8,128)(2,1)S(1)}, bf16[512,2048]{0,1:T(8,128)(2,1)S(1)}) fusion(bf16[512,2048]{0,1:T(8,128)(2,1)} %copy.91, bf16[512]{0:T(512)(128)(2,1)S(1)} %fusion.38, bf16[512,2048]{0,1:T(8,128)(2,1)} %copy.90, bf16[512,2048]{0,1:T(8,128)(2,1)} %copy.87), kind=kLoop, calls=%fused_computation.49 | loop fusion | flops 3145728 | bytes 12583936 | tf_op jit(solution)/shard_map/mul | solution.py:26
  34.8 2.1 fusion.45
  36.9 2.1 fusion.46
  39.1 90.9 %all-gather.3.cloned.1.call-done = f32[512,128,128]{2,1,0:T(8,128)} async-done(((f32[16,128,128]{2,1,0:T(8,128)}), f32[512,128,128]{2,1,0:T(8,128)}) %all-gather.3.cloned.1.call-update) | async-done | bytes 33554448 | tf_op jit(solution)/shard_map/all_gather | solution.py:14
  130.0 12.7 %reduce_sum.27 = f32[16,128,128]{2,1,0:T(8,128)} reduce(f32[32,16,128,128]{3,2,1,0:T(8,128)} %bitcast.122, f32[]{:T(128)} %constant.2.clone.1), dimensions={0}, to_apply=%region_0.0 | reduce | flops 8126464 | bytes 34603012 | tf_op jit(solution)/shard_map/reduce_sum | solution.py:14
  142.7 2.1 fusion.29
  144.8 2.3 add_bitcast_fusion.1
  150.6 8.6 %all-reduce = (f32[512]{0:T(512)S(1)}, f32[512]{0:T(512)S(1)}) all-reduce(f32[512]{0:T(512)S(1)} %get-tuple-element.28, f32[512]{0:T(512)S(1)} %fusion.2), channel_id=1, replica_groups=mesh['head'=4,'seq'=32] {'head'}, use_global_device_ids=true, to_apply=%region_2.0 | all-reduce | flops 1024 | bytes 8192 | tf_op jit(solution)/shard_map/psum | solution.py:72
  159.1 4.5 %fusion.5 = (bf16[512,2048]{0,1:T(8,128)(2,1)S(1)}, bf16[512,2048]{0,1:T(8,128)(2,1)}) fusion(f32[512,16,128]{0,2,1:T(8,128)} %copy-done.1, f32[512]{0:T(512)S(1)} %get-tuple-element.38, f32[512]{0:T(512)S(1)} %get-tuple-element.25, f32[512]{0:T(512)S(1)} %get-tuple-element.39, f32[2048]{0:T(1024)S(1)} %copy-done.36, bf16[512,2048]{0,1:T(8,128)(2,1)} %copy.99, ...), kind=kLoop, calls=%fused_computation.9 | loop fusion | flops 11534336 | bytes 10501120 | tf_op jit(solution)/shard_map/convert_element_type | solution.py:79
  163.8 2.2 copy-done.19
  169.2 1.8 fusion.51
  171.0 2.1 fusion.48
  173.1 1.8 fusion.52
  176.1 1.8 fusion.50
  177.9 2.1 fusion.47
  182.9 3.5 %fusion.27 = bf16[256,16,128]{0,2,1:T(8,128)(2,1)} fusion(f32[16,128,256]{2,1,0:T(8,128)} %fusion.52, bf16[256,16,128]{0,2,1:T(8,128)(2,1)S(1)} %bitcast.126, f32[16,128,128]{2,1,0:T(8,128)} %copy-done.22), kind=kOutput, calls=%fused_computation.44 | convolution fusion | flops 135528448 | bytes 5242880 | tf_op jit(solution)/shard_map/bhd,hde->bhe/dot_general | solution.py:97
  186.4 3.4 %fusion.26 = bf16[256,16,128]{0,2,1:T(8,128)(2,1)} fusion(f32[16,128,256]{2,1,0:T(8,128)} %fusion.51, bf16[256,16,128]{0,2,1:T(8,128)(2,1)} %bitcast.151), kind=kOutput, calls=%fused_computation.43 | convolution fusion | flops 135266304 | bytes 4194304 | tf_op jit(solution)/shard_map/bhe,hde->bhd/dot_general | solution.py:94
  196.7 3.9 %copy.120 = bf16[512,2048]{1,0:T(8,128)(2,1)} copy(bf16[512,2048]{0,1:T(8,128)(2,1)} %bitcast.153) | data formatting | bytes 4194304
  200.6 4.0 %copy.118 = bf16[512,2048]{1,0:T(8,128)(2,1)} copy(bf16[512,2048]{0,1:T(8,128)(2,1)} %bitcast.154) | data formatting | bytes 4194304
  204.6 2.4 fusion.25
  208.6 3.9 %copy.119 = bf16[512,2048]{1,0:T(8,128)(2,1)} copy(bf16[512,2048]{0,1:T(8,128)(2,1)} %bitcast.155) | data formatting | bytes 4194304
  212.5 3.9 %copy.117 = bf16[512,2048]{1,0:T(8,128)(2,1)} copy(bf16[512,2048]{0,1:T(8,128)(2,1)} %get-tuple-element.27) | data formatting | bytes 4194304
  216.4 73.7 %all-reduce.3.cloned.1.call-done = f32[16,128,128]{2,1,0:T(8,128)} async-done(((f32[16,128,128]{2,1,0:T(8,128)}), f32[16,128,128]{2,1,0:T(8,128)}) %all-reduce.3.cloned.1.call-update) | async-done | bytes 1048592 | tf_op jit(solution)/shard_map/psum | solution.py:121
  290.2 4.4 %fusion.13 = bf16[16,128,512]{2,1,0:T(8,128)(2,1)} fusion(f32[16,128,128]{2,1,0:T(8,128)} %all-reduce.3.cloned.1.call-done, bf16[512,2048]{1,0:T(8,128)(2,1)S(1)} %copy-done), kind=kOutput, calls=%fused_computation.34 | convolution fusion | flops 1611661312 | bytes 5242880 | tf_op jit(solution)/shard_map/thd,hde->the/dot_general | solution.py:127
  294.6 4.0 %copy.122 = bf16[512,2048]{1,0:T(8,128)(2,1)} copy(bf16[512,2048]{0,1:T(8,128)(2,1)} %bitcast.157) | data formatting | bytes 4194304
  298.6 4.8 %fusion.16 = bf16[16,128,512]{2,1,0:T(8,128)(2,1)} fusion(f32[16,128,128]{2,1,0:T(8,128)S(1)} %copy-done.32, bf16[512,2048]{1,0:T(8,128)(2,1)} %param.13), kind=kOutput, calls=%fused_computation.35 | convolution fusion | flops 1611661312 | bytes 5242880 | tf_op jit(solution)/shard_map/the,hde->thd/dot_general | solution.py:124
  303.4 3.9 %copy.121 = bf16[512,2048]{1,0:T(8,128)(2,1)} copy(bf16[512,2048]{0,1:T(8,128)(2,1)} %bitcast.156) | data formatting | bytes 4194304
  (99 shorter events, 23.4 us)
Async XLA Ops:
  7.2 1.6 copy-start
  7.2 122.8 %all-gather.3.cloned.1.call-start = ((), (), s32[]{:S(2)}) async-start(), calls=%async_computation.1 | async-start | bytes 34603008 | tf_op jit(solution)/shard_map/all_gather | solution.py:14
  12.2 277.9 %all-reduce.3.cloned.1.call-start = ((), (), s32[]{:S(2)}) async-start(), calls=%async_computation | async-start | bytes 2097152 | tf_op jit(solution)/shard_map/psum | solution.py:121
  32.5 1.5 copy-start.12
  32.5 2.2 copy-start.2
  32.5 4.4 %copy-start.25 = (bf16[256,2048]{0,1:T(8,128)(2,1)}, bf16[256,2048]{0,1:T(8,128)(2,1)S(1)}, u32[]{:S(2)}) copy-start(bf16[256,2048]{0,1:T(8,128)(2,1)S(1)} %get-tuple-element.43) | copy-start | bytes 3145732
  34.0 3.0 copy-start.18
  34.8 2.2 copy-start.16
  142.6 2.1 copy-start.13
  142.6 2.2 copy-start.20
  144.8 2.4 copy-start.30
  144.8 2.4 copy-start.10
  144.8 2.7 copy-start.29
  148.0 1.7 copy-start.15
  148.1 1.7 copy-start.36
  148.6 2.0 copy-start.1
  163.6 2.3 copy-start.19
  163.8 3.9 %copy-start.7 = (bf16[256,2048]{0,1:T(8,128)(2,1)}, bf16[256,2048]{0,1:T(8,128)(2,1)S(1)}, u32[]{:S(2)}) copy-start(bf16[256,2048]{0,1:T(8,128)(2,1)S(1)} %get-tuple-element.31) | copy-start | bytes 3145732
  163.8 17.7 %copy-start.5 = (bf16[256,2048]{0,1:T(8,128)(2,1)}, bf16[256,2048]{0,1:T(8,128)(2,1)S(1)}, u32[]{:S(2)}) copy-start(bf16[256,2048]{0,1:T(8,128)(2,1)S(1)} %get-tuple-element.30) | copy-start | bytes 3145732
  168.4 13.1 %copy-start.22 = (f32[16,128,128]{2,1,0:T(8,128)}, f32[16,128,128]{2,1,0:T(8,128)S(1)}, u32[]{:S(2)}) copy-start(f32[16,128,128]{2,1,0:T(8,128)S(1)} %fusion.49) | copy-start | bytes 3145732
  169.2 1.8 copy-start.24
  171.0 2.1 copy-start.17
  173.1 1.8 copy-start.3
  186.4 3.5 %copy-start.8 = (bf16[256,2048]{0,1:T(8,128)(2,1)S(1)}, bf16[256,2048]{0,1:T(8,128)(2,1)}, u32[]{:S(2)}) copy-start(bf16[256,2048]{0,1:T(8,128)(2,1)} %copy-done.7) | copy-start | bytes 3145732
  186.4 3.5 %copy-start.27 = (f32[16,128,256]{2,1,0:T(8,128)S(1)}, f32[16,128,256]{2,1,0:T(8,128)}, u32[]{:S(2)}) copy-start(f32[16,128,256]{2,1,0:T(8,128)} %fusion.48) | copy-start | bytes 6291460
  186.4 3.5 %copy-start.31 = (bf16[16,128,128]{2,1,0:T(8,128)(2,1)S(1)}, bf16[16,128,128]{2,1,0:T(8,128)(2,1)}, u32[]{:S(2)}) copy-start(bf16[16,128,128]{2,1,0:T(8,128)(2,1)} %copy-done.30) | copy-start | bytes 1572868
  189.9 1.5 copy-start.21
  189.9 2.2 copy-start.28
  192.1 1.6 copy-start.34
  200.6 4.0 %copy-start.4 = (bf16[256,2048]{0,1:T(8,128)(2,1)S(1)}, bf16[256,2048]{0,1:T(8,128)(2,1)}, u32[]{:S(2)}) copy-start(bf16[256,2048]{0,1:T(8,128)(2,1)} %copy-done.2) | copy-start | bytes 3145732
  204.6 2.4 copy-start.35
  294.6 4.0 %copy-start.32 = (f32[16,128,128]{2,1,0:T(8,128)S(1)}, f32[16,128,128]{2,1,0:T(8,128)}, u32[]{:S(2)}) copy-start(f32[16,128,128]{2,1,0:T(8,128)} %all-reduce.3.cloned.1.call-done) | copy-start | bytes 3145732
  (7 other events, 8.6 us)
Sparse Core Ops, SparseCore 0:
  12.3 117.5 all-gather.2
  186.5 103.5 all-reduce.2
